TPU v7x, 32 devices: a whole 2x2x4 slice. The times are simulated.
32 devices in a mesh: groups: 2 (over y), expert: 4 (over z), tensor: 4 (over x, core).
Axes of the slice: x: 2, y: 2, z: 4, core: 2. Of those that a mesh axis runs over, the one named last changes fastest.
Arguments:
- partials: bfloat16 [4, 512, 7168], P('tensor', ('groups', 'expert')), parts along dimension 1, may hold values from -6 to 6
- norm_gain: float32 [7168], replicated, may hold values from 0.1 to 1.9
- expert_ids: int32 [512, 8], P(('groups', 'expert')), parts along dimension 0, may hold values from 0 to 255, as said below
- gate_values: float32 [512, 8], P(('groups', 'expert')), parts along dimension 0, may hold values from 0.1 to 1
- up_weight: bfloat16 [4, 7168, 512], P('expert', None, 'tensor'), may hold values from -0.0625 to 0.0625
- down_weight: bfloat16 [4, 512, 7168], P('expert', 'tensor'), may hold values from -0.25 to 0.25
Outputs:
- routed: bfloat16 [512, 7168], P(('groups', 'expert', 'tensor')), parts along dimension 0
There are 2 independent parts, one for each index of `groups`. A program takes and returns all parts, laid end to end along the dimension named above; an argument that names none is the same for every part. Nothing has to cross between parts.
Inputs may be any that keep to these rules, and one draw needn't show every extreme that they name: `expert_ids`: each row names 8 different experts; only experts below 4 belong to the window. In each aligned block of 64 rows (one index of expert), a quarter of the window's experts are named exactly 4 times, a quarter 4 // 2 times and half 4 // 4 times; the quarter named 4 times is the same in every block.
All inputs are finite; a program needn't handle non-finite values.
Results may differ from a plain program's by a relative error of at most 0.018.
Values may be sent and summed in bfloat16 or wider, within the bound.
A program may use at most 64 MiB of HBM per device.

v0:
```python
import jax
import jax.numpy as jnp
from jax import lax
from jax.sharding import PartitionSpec as P

CAP = 4


def rms_norm(values, norm_gain):
    wide = values.astype(jnp.float32)
    mean_sq = jnp.mean(wide * wide, axis=-1, keepdims=True)
    return (wide * lax.rsqrt(mean_sq + 1e-06) * norm_gain).astype(jnp.bfloat16)


def slot_positions(expert_ids, n_owner):
    flat_ids = expert_ids.reshape(-1)
    onehot_table = (flat_ids[:, None] == jnp.arange(n_owner, dtype=jnp.int32)[None, :]).astype(
        jnp.int32
    )
    prior_result = jnp.cumsum(onehot_table, axis=0) - onehot_table
    rank_in = jnp.sum(prior_result * onehot_table, axis=1)
    inside = flat_ids < n_owner
    return jnp.where(inside, flat_ids * CAP + rank_in, -1).reshape(expert_ids.shape)


def on_device(partials, norm_gain, expert_ids, gate_values, up_weight, down_weight):
    n_expert = lax.axis_size("expert")
    row_width = partials.shape[2]
    slot_count = n_expert * CAP
    slot_of = slot_positions(expert_ids, n_expert)
    slot_grid = jnp.arange(slot_count, dtype=jnp.int32)
    matches = slot_of[None, :, :] == slot_grid[:, None, None]
    chooser = jnp.any(matches, axis=2).astype(jnp.bfloat16)
    weight_lookup = jnp.sum(jnp.where(matches, gate_values[None, :, :], 0.0), axis=2).T
    term_rows = partials[0]
    own_rows = (
        lax.psum_scatter(term_rows, "tensor", scatter_dimension=0, tiled=True)
        .astype(jnp.float32)
        .astype(jnp.bfloat16)
    )
    normed = lax.all_gather(rms_norm(own_rows, norm_gain), "tensor", axis=0, tiled=True)
    outgoing = jnp.dot(chooser, normed, preferred_element_type=jnp.float32).astype(jnp.bfloat16)
    arrived = lax.all_to_all(
        outgoing.reshape(n_expert, CAP, row_width),
        "expert",
        split_axis=0,
        concat_axis=0,
        tiled=True,
    )
    expert_rows = arrived.reshape(slot_count, row_width)
    up_proj = jnp.dot(expert_rows, up_weight[0], preferred_element_type=jnp.float32)
    hidden = jax.nn.silu(up_proj).astype(jnp.bfloat16)
    partial_down = jnp.dot(hidden, down_weight[0], preferred_element_type=jnp.float32).astype(
        jnp.bfloat16
    )
    summed = (
        lax.psum_scatter(partial_down, "tensor", scatter_dimension=1, tiled=True)
        .astype(jnp.float32)
        .astype(jnp.bfloat16)
    )
    returned = lax.all_to_all(
        summed.reshape(n_expert, CAP, summed.shape[1]),
        "expert",
        split_axis=0,
        concat_axis=0,
        tiled=True,
    )
    mixed_cols = jnp.dot(
        weight_lookup,
        returned.reshape(slot_count, -1).astype(jnp.float32),
        precision=lax.Precision.HIGHEST,
    ).astype(jnp.bfloat16)
    return lax.all_to_all(mixed_cols, "tensor", split_axis=0, concat_axis=1, tiled=True)


def solution(mesh):
    in_specs = (
        P("tensor", ("groups", "expert"), None),
        P(),
        P(("groups", "expert"), None),
        P(("groups", "expert"), None),
        P("expert", None, "tensor"),
        P("expert", "tensor", None),
    )
    out_specs = P(("groups", "expert", "tensor"), None)
    return jax.shard_map(
        on_device, mesh=mesh, in_specs=in_specs, out_specs=out_specs, check_vma=False
    )
```

profile of v0, /device:TPU:0, one launch (start us, length us, event | category | flops | bytes accessed | tf_op | source)
XLA Modules:
  0.0 110.6 jit_solution(4836795007789852619)
XLA Ops:
  6.5 0.0 copy-start
  6.5 0.0 reduce-scatter.3.cloned.1.call-start
  6.5 0.7 reduce-scatter.3.cloned.1.call-update
  7.3 0.0 reduce-scatter.5.cloned.1.call-start
  7.3 0.8 copy.26
  8.1 0.1 eq.42
  8.2 0.1 eq.38
  8.3 1.2 %reduce-window.6 = s32[4,4,128]{2,1,0:T(4,128)S(1)} reduce-window(s32[4,4,128]{2,1,0:T(4,128)S(1)} %fusion.14, s32[]{:T(128)} %constant.9.clone.1), window={size=1x1x128 pad=0_0x0_0x127_0}, to_apply=%region_0.0 | reduce-window | flops 260096 | bytes 16388 | tf_op jit(solution)/shard_map/reduce-window
  9.5 0.2 slice_reduce_fusion
  9.7 0.2 reduce-window.9
  9.9 0.1 add_bitcast_fusion
  10.0 0.1 reduce_sum.30
  10.1 0.1 copy.28
  10.2 0.7 add_select_fusion
  10.9 25.8 %reduce-scatter.3.cloned.1.call-done = bf16[16,7168]{1,0:T(8,128)(2,1)} async-done(((bf16[64,7168]{1,0:T(8,128)(2,1)}), bf16[16,7168]{1,0:T(8,128)(2,1)}) %reduce-scatter.3.cloned.1.call-update) | async-done | bytes 229392 | tf_op jit(solution)/shard_map/reduce_scatter | solution.py:37
  36.7 1.1 %fusion.3 = f32[16]{0:T(128)S(1)} fusion(bf16[16,7168]{1,0:T(8,128)(2,1)} %reduce-scatter.3.cloned.1.call-done), kind=kLoop, calls=%fused_computation.8 | loop fusion | flops 344048 | bytes 229440 | tf_op jit(solution)/shard_map/reduce_sum | solution.py:11
  37.8 1.1 fusion.5
  38.9 8.9 %all_gather.3 = bf16[64,7168]{1,0:T(8,128)(2,1)S(1)} all-gather(bf16[16,7168]{1,0:T(8,128)(2,1)S(1)} %fusion.5), channel_id=1, replica_groups=mesh['groups'=2,'expert'=4,'tensor'=4] {'tensor'}, dimensions={0}, use_global_device_ids=true | all-gather | bytes 1146880 | tf_op jit(solution)/shard_map/all_gather | solution.py:41
  47.8 0.2 convolution_convert_fusion.1
  48.1 0.1 reshape.52
  48.2 13.1 %all_to_all.29 = bf16[4,4,7168]{2,1,0:T(4,128)(2,1)S(1)} all-to-all(bf16[4,4,7168]{2,1,0:T(4,128)(2,1)S(1)} %reshape.52), channel_id=1, replica_groups=mesh['groups'=2,'expert'=4,'tensor'=4] {'expert'}, dimensions={0} | all-to-all | bytes 458752 | tf_op jit(solution)/shard_map/all_to_all | solution.py:43
  61.3 0.1 reshape.53
  61.3 0.0 copy-done
  61.3 0.0 copy-start.1
  61.3 2.9 %convolution_convert_fusion = bf16[16,7168]{1,0:T(8,128)(2,1)} fusion(bf16[1,128,7168]{2,1,0:T(8,128)(2,1)S(1)} %copy-done, bf16[16,7168]{1,0:T(8,128)(2,1)S(1)} %reshape.53, bf16[1,7168,128]{2,1,0:T(8,128)(2,1)} %param.10), kind=kOutput, calls=%fused_computation | convolution fusion | flops 58845184 | bytes 4128768 | tf_op jit(solution)/shard_map/dot_general | solution.py:53
  64.3 0.0 reduce-scatter.5.cloned.1.call-update
  64.3 18.5 %reduce-scatter.5.cloned.1.call-done = bf16[16,1792]{1,0:T(8,128)(2,1)} async-done(((bf16[16,7168]{1,0:T(8,128)(2,1)}), bf16[16,1792]{1,0:T(8,128)(2,1)}) %reduce-scatter.5.cloned.1.call-update) | async-done | bytes 57360 | tf_op jit(solution)/shard_map/reduce_scatter | solution.py:57
  82.8 1.5 %reshape.54 = bf16[4,4,1792]{2,1,0:T(4,128)(2,1)} reshape(bf16[16,1792]{1,0:T(8,128)(2,1)} %reduce-scatter.5.cloned.1.call-done) | data formatting | bytes 114688 | tf_op jit(solution)/shard_map/reshape | solution.py:62
  84.2 4.6 %all-to-all-start.1 = ((bf16[4,4,1792]{2,1,0:T(4,128)(2,1)}), bf16[4,4,1792]{2,1,0:T(4,128)(2,1)S(1)}, u32[]{:S(2)}, u32[]{:S(2)}) async-start(bf16[4,4,1792]{2,1,0:T(4,128)(2,1)} %reshape.54), calls=%async_computation.3 | async-start | bytes 114688 | tf_op jit(solution)/shard_map/all_to_all | solution.py:61
  88.8 0.0 copy-done.1
  88.9 5.7 %all-to-all-done.1 = bf16[4,4,1792]{2,1,0:T(4,128)(2,1)S(1)} async-done(((bf16[4,4,1792]{2,1,0:T(4,128)(2,1)}), bf16[4,4,1792]{2,1,0:T(4,128)(2,1)S(1)}, u32[]{:S(2)}, u32[]{:S(2)}) %all-to-all-start.1) | async-done | bytes 57376 | tf_op jit(solution)/shard_map/all_to_all | solution.py:61
  94.6 0.4 convolution_convert_fusion.2
  95.0 8.1 %all_to_all.30 = bf16[4,16,1792]{2,1,0:T(8,128)(2,1)S(1)} all-to-all(bf16[4,16,1792]{2,1,0:T(8,128)(2,1)S(1)} %bitcast.40), channel_id=1, replica_groups=mesh['groups'=2,'expert'=4,'tensor'=4] {'tensor'}, dimensions={0} | all-to-all | bytes 458752 | tf_op jit(solution)/shard_map/all_to_all | solution.py:73
  103.0 0.7 copy.30
  (6 shorter events, 0.1 us)
Async XLA Ops:
  6.5 54.8 %copy-start = (bf16[1,128,7168]{2,1,0:T(8,128)(2,1)S(1)}, bf16[1,128,7168]{2,1,0:T(8,128)(2,1)}, u32[]{:S(2)}) copy-start(bf16[1,128,7168]{2,1,0:T(8,128)(2,1)} %param.11) | copy-start | bytes 5505028
  6.5 30.2 %reduce-scatter.3.cloned.1.call-start = ((), (), s32[]{:S(2)}) async-start(), calls=%async_computation.5 | async-start | bytes 1146880 | tf_op jit(solution)/shard_map/reduce_scatter | solution.py:37
  7.3 75.5 %reduce-scatter.5.cloned.1.call-start = ((), (), s32[]{:S(2)}) async-start(), calls=%async_computation.6 | async-start | bytes 286720 | tf_op jit(solution)/shard_map/reduce_scatter | solution.py:57
  61.3 27.5 %copy-start.1 = (f32[64,8]{0,1:T(8,128)S(1)}, f32[64,8]{0,1:T(8,128)}, u32[]{:S(2)}) copy-start(f32[64,8]{0,1:T(8,128)} %param.9) | copy-start | bytes 6148
  84.2 10.3 %all-to-all-start.1 = ((bf16[4,4,1792]{2,1,0:T(4,128)(2,1)}), bf16[4,4,1792]{2,1,0:T(4,128)(2,1)S(1)}, u32[]{:S(2)}, u32[]{:S(2)}) async-start(bf16[4,4,1792]{2,1,0:T(4,128)(2,1)} %reshape.54), calls=%async_computation.3 | async-start | bytes 114688 | tf_op jit(solution)/shard_map/all_to_all | solution.py:61
Sparse Core Ops, SparseCore 0:
  9.9 26.7 reduce-scatter.2
  64.4 18.3 reduce-scatter.4
where the time goes:
time: 111 us
  waiting for transfers between devices  50.7 us (46%)
  blocking collectives  30.1 us (27%)
  between operations  13.5 us (12%)
  starting transfers between devices  4.65 us (4%)
  other arithmetic  4.47 us (4%)
  local copies, waits for them, and re-layouts  3.66 us (3%)
  matrix products  3.53 us (3%)
    reduce_scatter x1, waiting for transfers between devices, on_device(): lax.psum_scatter(term_rows, 'tensor', scatter_dimension=0, tiled=True)  25.8 us
    reduce_scatter x1, waiting for transfers between devices, on_device(): lax.psum_scatter(partial_down, 'tensor', scatter_dimension=1, tiled=True)  18.5 us
    all_to_all x1, blocking collectives, on_device(): lax.all_to_all(outgoing.reshape(n_expert, CAP, row_width), 'expert', spli...  13.1 us
    all_gather x1, blocking collectives, on_device(): lax.all_gather(rms_norm(own_rows, norm_gain), 'tensor', axis=0, tiled=True)  8.92 us
    all_to_all x1, blocking collectives, on_device(): lax.all_to_all(mixed_cols, 'tensor', split_axis=0, concat_axis=1, tiled=T...  8.06 us
    all_to_all x1, waiting for transfers between devices, on_device(): lax.all_to_all(summed.reshape(n_expert, CAP, summed.shape[1]), 'expert',...  5.69 us
    all_to_all x1, starting transfers between devices, on_device(): lax.all_to_all(summed.reshape(n_expert, CAP, summed.shape[1]), 'expert',...  4.61 us
    dot_general x1, matrix products, on_device(): jnp.dot(hidden, down_weight[0], preferred_element_type=jnp.float32)  2.91 us
  transfers between devices with their start and end apart: 3, of which 3 were waited for; matrix products, arithmetic and copies ran while one was open for 3% of the time, Pallas kernels for 0%

commit v1 on v0

v1 whole, which is shorter than its diff:
```python
import functools

import jax
import jax.numpy as jnp
from jax import lax
from jax.experimental import pallas as pl
from jax.experimental.pallas import tpu as pltpu
from jax.sharding import PartitionSpec as P

CAP = 4
CUTS = 4
GRP = CAP * CUTS
MESH = pl.DeviceIdType.MESH
F32 = jnp.float32
BF16 = jnp.bfloat16


def iota(shape, dim):
    return lax.broadcasted_iota(jnp.int32, shape, dim)


def nt_dot(a, b):
    return lax.dot_general(a, b, (((1,), (1,)), ((), ())), preferred_element_type=F32)


def nn_dot(a, b):
    return jnp.dot(a, b, preferred_element_type=F32)


def kernel(
    dims,
    part_hbm,
    gain_hbm,
    ids_hbm,
    gate_hbm,
    up_hbm,
    down_hbm,
    out_ref,
    part_v,
    gain_v,
    ids_v,
    gate_v,
    up_v,
    down_v,
    gain_rows,
    spread,
    send1,
    recv1,
    send2,
    xbuf,
    send3,
    recv3,
    send4,
    recv4,
    recv5,
    load_sem,
    s1,
    r1,
    s2,
    r2,
    s2b,
    r2b,
    s3,
    r3,
    s4,
    r4,
    s5,
    r5,
):
    n_e, n_t, rows, width = dims
    ff = up_hbm.shape[2]
    chunk = width // CUTS
    lanes = send1.shape[2]
    picks = 2 * n_e
    crow = CUTS * picks
    own = rows // n_t
    srow = n_e * GRP
    me_e = lax.axis_index("expert")
    me_t = lax.axis_index("tensor")
    t_order = sorted(range(1, n_t), key=lambda j: -min(j, n_t - j))
    e_order = sorted(range(1, n_e), key=lambda j: -min(j, n_e - j))
    t_peers = [lax.rem(me_t + j, n_t) for j in t_order]
    e_peers = [lax.rem(me_e + j, n_e) for j in e_order]

    barrier = pltpu.get_barrier_semaphore()
    for peer in t_peers:
        pl.semaphore_signal(barrier, inc=1, device_id={"tensor": peer}, device_id_type=MESH)
    for peer in e_peers:
        pl.semaphore_signal(barrier, inc=1, device_id={"expert": peer}, device_id_type=MESH)

    small = [
        pltpu.make_async_copy(ids_hbm, ids_v, load_sem.at[0]),
        pltpu.make_async_copy(gate_hbm, gate_v, load_sem.at[1]),
    ]
    parts = [
        pltpu.make_async_copy(
            part_hbm.at[0, :, pl.ds(c * chunk, chunk)],
            part_v.at[pl.ds(c * rows, rows), :],
            load_sem.at[2 + c],
        )
        for c in range(CUTS)
    ]
    gain_copy = pltpu.make_async_copy(gain_hbm, gain_v, load_sem.at[2 + CUTS])
    ups = [
        pltpu.make_async_copy(
            up_hbm.at[0, pl.ds(c * chunk, chunk), :],
            up_v.at[:, pl.ds(c * ff, ff)],
            load_sem.at[3 + CUTS + c],
        )
        for c in range(CUTS)
    ]
    downs = [
        pltpu.make_async_copy(
            down_hbm.at[0, :, pl.ds(c * chunk, chunk)],
            down_v.at[pl.ds(c * ff, ff), :],
            load_sem.at[3 + 2 * CUTS + c],
        )
        for c in range(CUTS)
    ]
    for copy in small + parts + [gain_copy] + ups + downs:
        copy.start()
    for copy in small:
        copy.wait()

    slot_l = max(128, srow)
    pick_l = max(128, crow)
    lane = iota((rows, slot_l), 1)
    lane_e = lane // GRP
    lane_s = lane % CAP
    named = jnp.zeros((rows, slot_l), F32)
    gates = jnp.zeros((rows, slot_l), F32)
    for k in range(ids_v.shape[1]):
        hit = (ids_v[:, k : k + 1] == lane_e) & (lane < srow)
        named = named + jnp.where(hit, 1.0, 0.0)
        gates = gates + jnp.where(hit, gate_v[:, k : k + 1], 0.0)
    before = (iota((rows, rows), 0) > iota((rows, rows), 1)).astype(F32).astype(BF16)
    rank = nn_dot(before, named.astype(BF16)).astype(jnp.int32)
    in_slot = jnp.where(rank == lane_s, named, 0.0)
    slot_gate = in_slot * gates
    any_hit = jnp.broadcast_to(jnp.max(named, axis=1, keepdims=True), (rows, pick_l))
    place = nn_dot(before, any_hit.astype(BF16)).astype(jnp.int32)
    lane_p = iota((rows, pick_l), 1)
    picked = jnp.where((place == lane_p % picks) & (lane_p < crow), any_hit, 0.0).astype(BF16)
    spread[...] = picked.astype(F32)

    pick_row = (iota((crow, pick_l), 0) == iota((crow, pick_l), 1)).astype(F32).astype(BF16)
    pick_t = nt_dot(pick_row, picked)
    stacked = jnp.concatenate([picked] * CUTS, axis=0)
    wide = nt_dot(pick_row, stacked)
    chooser = jnp.where(
        iota((crow, CUTS * rows), 0) // picks == iota((crow, CUTS * rows), 1) // rows, wide, 0.0
    ).astype(BF16)

    for copy in parts:
        copy.wait()
    for t in range(n_t):
        lo, hi = min(t * lanes, chunk), min((t + 1) * lanes, chunk)
        if hi - lo < lanes:
            send1[t] = jnp.zeros((crow, lanes), BF16)
        if hi > lo:
            send1[t, :, : hi - lo] = nn_dot(chooser, part_v[:, lo:hi]).astype(BF16)

    pl.semaphore_wait(barrier, len(t_peers) + len(e_peers))

    def copy1(src_t, dst_t):
        return pltpu.make_async_remote_copy(
            src_ref=send1.at[dst_t],
            dst_ref=recv1.at[src_t],
            send_sem=s1.at[dst_t],
            recv_sem=r1.at[src_t],
            device_id={"tensor": dst_t},
            device_id_type=MESH,
        )

    for peer in t_peers:
        copy1(me_t, peer).start()

    slot_row = (iota((srow, slot_l), 0) == iota((srow, slot_l), 1)).astype(F32).astype(BF16)
    slot_t = nt_dot(slot_row, in_slot.astype(BF16)).astype(BF16)
    to_slots = nn_dot(slot_t, picked)
    to_slots = jnp.where(
        (iota((srow, pick_l), 0) % GRP) // CAP == iota((srow, pick_l), 1) // picks, to_slots, 0.0
    )[:, :crow].astype(BF16)
    mix = jnp.dot(pick_t, slot_gate, preferred_element_type=F32, precision=lax.Precision.HIGHEST)
    mix = jnp.where(
        iota((crow, slot_l), 0) // picks == (iota((crow, slot_l), 1) % GRP) // CAP, mix, 0.0
    )[:, :srow]
    mix_hi = mix.astype(BF16)
    mix_lo = (mix - mix_hi.astype(F32)).astype(BF16)
    gain_copy.wait()
    row_c = iota((GRP, chunk), 0) // CAP
    spread_gain = jnp.broadcast_to(gain_v[:, :chunk], (GRP, chunk))
    for c in range(1, CUTS):
        spread_gain = jnp.where(
            row_c == c,
            jnp.broadcast_to(gain_v[:, c * chunk : (c + 1) * chunk], (GRP, chunk)),
            spread_gain,
        )
    gain_rows[...] = spread_gain

    total = send1[me_t].astype(F32)
    for peer in t_peers:
        copy1(peer, me_t).wait_recv()
        total = total + recv1[peer].astype(F32)
    attended = total.astype(BF16)
    slots = nn_dot(to_slots, attended).astype(BF16)
    for e in range(n_e):
        send2[e] = slots[e * GRP : (e + 1) * GRP]

    def xpart(b, t):
        return xbuf.at[
            pl.ds(pl.multiple_of(b * GRP, GRP), GRP), pl.ds(pl.multiple_of(t * lanes, 128), lanes)
        ]

    def copy2(src_e, dst_e):
        return pltpu.make_async_remote_copy(
            src_ref=send2.at[dst_e],
            dst_ref=xpart(src_e, me_t),
            send_sem=s2.at[dst_e],
            recv_sem=r2.at[src_e],
            device_id={"expert": dst_e},
            device_id_type=MESH,
        )

    def copy2b(b, src_t, dst_t):
        return pltpu.make_async_remote_copy(
            src_ref=xpart(b, src_t),
            dst_ref=xpart(b, src_t),
            send_sem=s2b.at[b, dst_t],
            recv_sem=r2b.at[b, src_t],
            device_id={"tensor": dst_t},
            device_id_type=MESH,
        )

    for peer in e_peers:
        copy2(me_e, peer).start()
    xpart(me_e, me_t)[...] = send2[me_e]
    for peer in t_peers:
        copy2b(me_e, me_t, peer).start()
    for src in e_peers[::-1]:
        copy2(src, me_e).wait_recv()
        for peer in t_peers:
            copy2b(src, me_t, peer).start()
    for copy in ups:
        copy.wait()
    for src in t_peers[::-1]:
        for b in [me_e] + e_peers[::-1]:
            copy2b(b, src, me_t).wait_recv()

    rows_x = xbuf[:, :chunk].astype(F32)
    square = jnp.sum(rows_x * rows_x, axis=1, keepdims=True)
    scaled = (rows_x.reshape(n_e, GRP, chunk) * gain_rows[...][None]).reshape(srow, chunk)
    up_all = nn_dot(scaled.astype(BF16), up_v[...])
    own_c = (iota((srow, ff), 0) % GRP) // CAP
    up_own = up_all[:, :ff]
    for c in range(1, CUTS):
        up_own = jnp.where(own_c == c, up_all[:, c * ff : (c + 1) * ff], up_own)
    joined = jnp.concatenate([up_own, jnp.broadcast_to(square, (srow, ff))], axis=1)
    r_i, c_i = iota((srow, srow), 0), iota((srow, srow), 1)
    same = ((r_i // GRP == c_i // GRP) & (r_i % CAP == c_i % CAP)).astype(F32)
    summed = jnp.dot(same, joined, preferred_element_type=F32, precision=lax.Precision.HIGHEST)
    up_proj = summed[:, :ff] * lax.rsqrt(summed[:, ff:] * (1.0 / width) + 1e-06)
    hidden = up_proj / (1.0 + jnp.exp(-up_proj))
    spread_h = jnp.concatenate(
        [jnp.where(own_c == c, hidden, 0.0).astype(BF16) for c in range(CUTS)], axis=1
    )
    for copy in downs:
        copy.wait()

    def copy3(src_t, dst_t):
        return pltpu.make_async_remote_copy(
            src_ref=send3.at[dst_t],
            dst_ref=recv3.at[src_t],
            send_sem=s3.at[dst_t],
            recv_sem=r3.at[src_t],
            device_id={"tensor": dst_t},
            device_id_type=MESH,
        )

    for t in range(n_t):
        lo, hi = min(t * lanes, chunk), min((t + 1) * lanes, chunk)
        if hi - lo < lanes:
            send3[t] = jnp.zeros((srow, lanes), BF16)
        if hi > lo:
            send3[t, :, : hi - lo] = nn_dot(spread_h, down_v[:, lo:hi]).astype(BF16)
    for peer in t_peers:
        copy3(me_t, peer).start()

    total = send3[me_t].astype(F32)
    for peer in t_peers[::-1]:
        copy3(peer, me_t).wait_recv()
        total = total + recv3[peer].astype(F32)
    send4[...] = total.astype(BF16).reshape(n_e, GRP, lanes)

    def copy4(src_e, dst_e):
        return pltpu.make_async_remote_copy(
            src_ref=send4.at[dst_e],
            dst_ref=recv4.at[src_e],
            send_sem=s4.at[dst_e],
            recv_sem=r4.at[src_e],
            device_id={"expert": dst_e},
            device_id_type=MESH,
        )

    for peer in e_peers:
        copy4(me_e, peer).start()
    recv4[me_e] = send4[me_e]
    for peer in e_peers[::-1]:
        copy4(peer, me_e).wait_recv()
    pairs = recv4[...].reshape(srow, lanes)
    mixed = nn_dot(mix_hi, pairs) + nn_dot(mix_lo, pairs)
    recv5[me_t] = mixed.astype(BF16)

    def copy5(src_t, dst_t):
        return pltpu.make_async_remote_copy(
            src_ref=recv5.at[src_t],
            dst_ref=recv5.at[src_t],
            send_sem=s5.at[dst_t],
            recv_sem=r5.at[src_t],
            device_id={"tensor": dst_t},
            device_id_type=MESH,
        )

    for peer in t_peers:
        copy5(me_t, peer).start()

    mine = spread[pl.ds(pl.multiple_of(me_t * own, own), own), :]
    home = jnp.concatenate([mine] * CUTS, axis=0)
    home = jnp.where(
        iota((CUTS * own, pick_l), 0) // own == iota((CUTS * own, pick_l), 1) // picks, home, 0.0
    )[:, :crow].astype(BF16)
    for peer in t_peers[::-1]:
        copy5(peer, me_t).wait_recv()
    for t in range(n_t):
        lo, hi = min(t * lanes, chunk), min((t + 1) * lanes, chunk)
        if hi > lo:
            block = nn_dot(home, recv5[t]).astype(BF16)
            for c in range(CUTS):
                out_ref[:, c * chunk + lo : c * chunk + hi] = block[
                    c * own : (c + 1) * own, : hi - lo
                ]

    for peer in t_peers:
        copy1(me_t, peer).wait_send()
        copy3(me_t, peer).wait_send()
        copy5(me_t, peer).wait_send()
        for b in [me_e] + e_peers:
            copy2b(b, me_t, peer).wait_send()
    for peer in e_peers:
        copy2(me_e, peer).wait_send()
        copy4(me_e, peer).wait_send()


def on_device(partials, norm_gain, expert_ids, gate_values, up_weight, down_weight):
    n_e, n_t = lax.axis_size("expert"), lax.axis_size("tensor")
    rows, width = partials.shape[1:]
    ff = up_weight.shape[2]
    chunk = width // CUTS
    lanes = -(-(chunk // 128) // n_t) * 128
    crow = CUTS * 2 * n_e
    srow = n_e * GRP
    own = rows // n_t
    dma = pltpu.SemaphoreType.DMA
    return pl.pallas_call(
        functools.partial(kernel, (n_e, n_t, rows, width)),
        out_shape=jax.ShapeDtypeStruct((own, width), BF16),
        in_specs=[pl.BlockSpec(memory_space=pl.ANY)] * 6,
        out_specs=pl.BlockSpec(memory_space=pltpu.VMEM),
        scratch_shapes=[
            pltpu.VMEM((CUTS * rows, chunk), BF16),
            pltpu.VMEM((1, width), F32),
            pltpu.VMEM(expert_ids.shape, jnp.int32),
            pltpu.VMEM(gate_values.shape, F32),
            pltpu.VMEM((chunk, CUTS * ff), BF16),
            pltpu.VMEM((CUTS * ff, chunk), BF16),
            pltpu.VMEM((GRP, chunk), F32),
            pltpu.VMEM((rows, max(128, crow)), F32),
            pltpu.VMEM((n_t, crow, lanes), BF16),
            pltpu.VMEM((n_t, crow, lanes), BF16),
            pltpu.VMEM((n_e, GRP, lanes), BF16),
            pltpu.VMEM((srow, n_t * lanes), BF16),
            pltpu.VMEM((n_t, srow, lanes), BF16),
            pltpu.VMEM((n_t, srow, lanes), BF16),
            pltpu.VMEM((n_e, GRP, lanes), BF16),
            pltpu.VMEM((n_e, GRP, lanes), BF16),
            pltpu.VMEM((n_t, crow, lanes), BF16),
            dma((3 + 3 * CUTS,)),
            dma((n_t,)),
            dma((n_t,)),
            dma((n_e,)),
            dma((n_e,)),
            dma((n_e, n_t)),
            dma((n_e, n_t)),
            dma((n_t,)),
            dma((n_t,)),
            dma((n_e,)),
            dma((n_e,)),
            dma((n_t,)),
            dma((n_t,)),
        ],
        compiler_params=pltpu.CompilerParams(
            collective_id=0, has_side_effects=True, vmem_limit_bytes=48 * 1024 * 1024
        ),
    )(partials, norm_gain.reshape(1, width), expert_ids, gate_values, up_weight, down_weight)


def solution(mesh):
    in_specs = (
        P("tensor", ("groups", "expert"), None),
        P(),
        P(("groups", "expert"), None),
        P(("groups", "expert"), None),
        P("expert", None, "tensor"),
        P("expert", "tensor", None),
    )
    out_specs = P(("groups", "expert", "tensor"), None)
    return jax.shard_map(
        on_device, mesh=mesh, in_specs=in_specs, out_specs=out_specs, check_vma=False
    )
```

time: 111 us -> 36.2 us (0.33)
  waiting for transfers between devices: 50.7 us -> 0 us
  blocking collectives: 30.1 us -> 0 us
  Pallas kernels: 0 us -> 28.7 us
  between operations: 13.5 us -> 0.01 us
  starting transfers between devices: 4.65 us -> 0 us
  other arithmetic: 4.47 us -> 0 us
  matrix products: 3.53 us -> 0 us
  local copies, waits for them, and re-layouts: 3.66 us -> 7.15 us
    reduce_scatter x2 -> x0, waiting for transfers between devices: 44.3 us -> none  [the longest x1 25.8 us: on_device(): lax.psum_scatter(term_rows, 'tensor', scatter_dimension=0, tiled=True)]
    pallas_call x0 -> x1, Pallas kernels: none -> 28.7 us  [on_device(): pl.pallas_call(functools.partial(kernel, (n_e, n_t, rows, width)), out_sh...]
    all_to_all x2 -> x0, blocking collectives: 21.2 us -> none  [the longest x1 13.1 us: on_device(): lax.all_to_all(outgoing.reshape(n_expert, CAP, row_width), 'expert', spli...]
    all_gather x1 -> x0, blocking collectives: 8.92 us -> none  [on_device(): lax.all_gather(rms_norm(own_rows, norm_gain), 'tensor', axis=0, tiled=True)]
    unnamed x5 -> x11, local copies, waits for them, and re-layouts: 0.78 us -> 7.15 us
    all_to_all x1 -> x0, waiting for transfers between devices: 5.69 us -> none  [on_device(): lax.all_to_all(summed.reshape(n_expert, CAP, summed.shape[1]), 'expert',...]
    all_to_all x1 -> x0, starting transfers between devices: 4.61 us -> none  [on_device(): lax.all_to_all(summed.reshape(n_expert, CAP, summed.shape[1]), 'expert',...]
    dot_general x3 -> x0, matrix products: 3.53 us -> none  [the longest x1 2.91 us: on_device(): jnp.dot(hidden, down_weight[0], preferred_element_type=jnp.float32)]
  transfers between devices with their start and end apart: 3 -> 0, of which waited for: 3 -> 0; matrix products, arithmetic and copies ran while one was open for 3% -> 0% of each run, Pallas kernels for 0% -> 0%
where the time goes in v1:
time: 36.2 us; the launch traced here: 35.9 us
  Pallas kernels  28.7 us (79%)
  local copies, waits for them, and re-layouts  7.15 us (20%)
    pallas_call x1, Pallas kernels, on_device(): pl.pallas_call(functools.partial(kernel, (n_e, n_t, rows, width)), out_sh...  28.7 us
    unnamed x11, local copies, waits for them, and re-layouts  7.15 us

profile of v1, /device:TPU:0, one launch (start us, length us, event | category | flops | bytes accessed | tf_op | source)
XLA Modules:
  0.0 35.9 jit_solution(8768384237217489417)
XLA Ops:
  0.0 0.8 %copy.7.ids_hbm = s32[64,8]{1,0:T(8,128)S(1)} copy(s32[64,8]{0,1:T(8,128)} %param.8) | data formatting | bytes 4096 | tf_op args[2]
  0.8 0.8 %copy.8.gate_hbm = f32[64,8]{1,0:T(8,128)S(1)} copy(f32[64,8]{0,1:T(8,128)} %param.9) | data formatting | bytes 4096 | tf_op args[3]
  1.5 0.0 copy-start
  1.5 1.5 %copy-done = bf16[1,7168,128]{2,1,0:T(8,128)(2,1)S(1)} copy-done((bf16[1,7168,128]{2,1,0:T(8,128)(2,1)S(1)}, bf16[1,7168,128]{2,1,0:T(8,128)(2,1)}, u32[]{:S(2)}) %copy-start) | copy-done | bytes 1835032
  3.0 0.0 copy-start.1
  3.0 1.5 %copy-done.1 = bf16[1,128,7168]{2,1,0:T(8,128)(2,1)S(1)} copy-done((bf16[1,128,7168]{2,1,0:T(8,128)(2,1)S(1)}, bf16[1,128,7168]{2,1,0:T(8,128)(2,1)}, u32[]{:S(2)}) %copy-start.1) | copy-done | bytes 1835032
  4.5 0.0 copy-start.2
  4.5 1.2 %copy-done.2 = bf16[1,64,7168]{2,1,0:T(8,128)(2,1)S(1)} copy-done((bf16[1,64,7168]{2,1,0:T(8,128)(2,1)S(1)}, bf16[1,64,7168]{2,1,0:T(8,128)(2,1)}, u32[]{:S(2)}) %copy-start.2) | copy-done | bytes 917528
  5.7 0.0 copy-start.3
  5.7 0.7 %copy-done.3 = f32[7168]{0:T(1024)S(1)} copy-done((f32[7168]{0:T(1024)S(1)}, f32[7168]{0:T(1024)}, u32[]{:S(2)}) %copy-start.3) | copy-done | bytes 28696
  6.5 28.7 %shard_map.64 = bf16[16,7168]{1,0:T(8,128)(2,1)S(1)} custom-call(bf16[1,64,7168]{2,1,0:T(8,128)(2,1)S(1)} %copy-done.2, f32[1,7168]{1,0:T(1,128)S(1)} %bitcast.1, s32[64,8]{1,0:T(8,128)S(1)} %copy.7.ids_hbm, f32[64,8]{1,0:T(8,128)S(1)} %copy.8.gate_hbm, bf16[1,7168,128]{2,1,0:T(8,128)(2,1)S(1)} %copy-done, bf16[1,128,7168]{2,1,0:T(8,128)(2,1)S(1)} %copy-done.1), custom_call_target="tpu_custom_call" | custom-call | tf_op jit(solution)/shard_map/pallas_call | solution.py:364
  35.2 0.7 %copy.10 = bf16[16,7168]{1,0:T(8,128)(2,1)} copy(bf16[16,7168]{1,0:T(8,128)(2,1)S(1)} %shard_map.64) | data formatting | bytes 458752
Async XLA Ops:
  1.5 1.5 %copy-start = (bf16[1,7168,128]{2,1,0:T(8,128)(2,1)S(1)}, bf16[1,7168,128]{2,1,0:T(8,128)(2,1)}, u32[]{:S(2)}) copy-start(bf16[1,7168,128]{2,1,0:T(8,128)(2,1)} %up_hbm.1) | copy-start | bytes 5505028
  3.0 1.5 %copy-start.1 = (bf16[1,128,7168]{2,1,0:T(8,128)(2,1)S(1)}, bf16[1,128,7168]{2,1,0:T(8,128)(2,1)}, u32[]{:S(2)}) copy-start(bf16[1,128,7168]{2,1,0:T(8,128)(2,1)} %down_hbm.1) | copy-start | bytes 5505028
  4.5 1.2 %copy-start.2 = (bf16[1,64,7168]{2,1,0:T(8,128)(2,1)S(1)}, bf16[1,64,7168]{2,1,0:T(8,128)(2,1)}, u32[]{:S(2)}) copy-start(bf16[1,64,7168]{2,1,0:T(8,128)(2,1)} %part_hbm.1) | copy-start | bytes 2752516
  5.7 0.7 %copy-start.3 = (f32[7168]{0:T(1024)S(1)}, f32[7168]{0:T(1024)}, u32[]{:S(2)}) copy-start(f32[7168]{0:T(1024)} %param.7) | copy-start | bytes 86020

commit v2 on v1

--- a/solution.py
+++ b/solution.py
@@ -17,6 +17,14 @@
 
 def iota(shape, dim):
     return lax.broadcasted_iota(jnp.int32, shape, dim)
+
+
+def div(x, n):
+    return x >> (n.bit_length() - 1) if n & (n - 1) == 0 else x // n
+
+
+def mod(x, n):
+    return x & (n - 1) if n & (n - 1) == 0 else x % n
 
 
 def nt_dot(a, b):
@@ -43,7 +51,6 @@
     up_v,
     down_v,
     gain_rows,
-    spread,
     send1,
     recv1,
     send2,
@@ -122,33 +129,27 @@
     for copy in small:
         copy.wait()
 
-    slot_l = max(128, srow)
-    pick_l = max(128, crow)
-    lane = iota((rows, slot_l), 1)
-    lane_e = lane // GRP
-    lane_s = lane % CAP
-    named = jnp.zeros((rows, slot_l), F32)
-    gates = jnp.zeros((rows, slot_l), F32)
-    for k in range(ids_v.shape[1]):
-        hit = (ids_v[:, k : k + 1] == lane_e) & (lane < srow)
-        named = named + jnp.where(hit, 1.0, 0.0)
-        gates = gates + jnp.where(hit, gate_v[:, k : k + 1], 0.0)
-    before = (iota((rows, rows), 0) > iota((rows, rows), 1)).astype(F32).astype(BF16)
-    rank = nn_dot(before, named.astype(BF16)).astype(jnp.int32)
-    in_slot = jnp.where(rank == lane_s, named, 0.0)
-    slot_gate = in_slot * gates
-    any_hit = jnp.broadcast_to(jnp.max(named, axis=1, keepdims=True), (rows, pick_l))
-    place = nn_dot(before, any_hit.astype(BF16)).astype(jnp.int32)
-    lane_p = iota((rows, pick_l), 1)
-    picked = jnp.where((place == lane_p % picks) & (lane_p < crow), any_hit, 0.0).astype(BF16)
-    spread[...] = picked.astype(F32)
-
-    pick_row = (iota((crow, pick_l), 0) == iota((crow, pick_l), 1)).astype(F32).astype(BF16)
-    pick_t = nt_dot(pick_row, picked)
-    stacked = jnp.concatenate([picked] * CUTS, axis=0)
-    wide = nt_dot(pick_row, stacked)
+    slot_r = iota((srow, rows), 0)
+    slot_e = div(slot_r, GRP)
+    named = jnp.zeros((srow, rows), F32)
+    gates = jnp.zeros((srow, rows), F32)
+    for k in range(ids_v.shape[0]):
+        hit = ids_v[k : k + 1, :] == slot_e
+        named = jnp.where(hit, 1.0, named)
+        gates = jnp.where(hit, gate_v[k : k + 1, :], gates)
+    before = (iota((rows, rows), 0) < iota((rows, rows), 1)).astype(F32).astype(BF16)
+    any_hit = jnp.broadcast_to(jnp.max(named, axis=0, keepdims=True), (crow, rows))
+    counts = nn_dot(jnp.concatenate([any_hit, named], axis=0).astype(BF16), before)
+    pick_r = mod(iota((crow, rows), 0), picks).astype(F32)
+    picked = jnp.where(counts[:crow] == pick_r, any_hit, 0.0)
+    pick_b = picked.astype(BF16)
+    rank = counts[crow:]
+    repeat = iota((rows, CUTS * rows), 0) == mod(iota((rows, CUTS * rows), 1), rows)
+    wide = nn_dot(pick_b, repeat.astype(F32).astype(BF16))
     chooser = jnp.where(
-        iota((crow, CUTS * rows), 0) // picks == iota((crow, CUTS * rows), 1) // rows, wide, 0.0
+        div(iota((crow, CUTS * rows), 0), picks) == div(iota((crow, CUTS * rows), 1), rows),
+        wide,
+        0.0,
     ).astype(BF16)
 
     for copy in parts:
@@ -175,20 +176,33 @@
     for peer in t_peers:
         copy1(me_t, peer).start()
 
-    slot_row = (iota((srow, slot_l), 0) == iota((srow, slot_l), 1)).astype(F32).astype(BF16)
-    slot_t = nt_dot(slot_row, in_slot.astype(BF16)).astype(BF16)
-    to_slots = nn_dot(slot_t, picked)
+    in_slot = jnp.where(rank == mod(slot_r, CAP).astype(F32), named, 0.0)
     to_slots = jnp.where(
-        (iota((srow, pick_l), 0) % GRP) // CAP == iota((srow, pick_l), 1) // picks, to_slots, 0.0
-    )[:, :crow].astype(BF16)
-    mix = jnp.dot(pick_t, slot_gate, preferred_element_type=F32, precision=lax.Precision.HIGHEST)
+        div(mod(iota((srow, crow), 0), GRP), CAP) == div(iota((srow, crow), 1), picks),
+        nt_dot(in_slot.astype(BF16), pick_b),
+        0.0,
+    ).astype(BF16)
+    mix = lax.dot_general(
+        picked,
+        in_slot * gates,
+        (((1,), (1,)), ((), ())),
+        preferred_element_type=F32,
+        precision=lax.Precision.HIGHEST,
+    )
     mix = jnp.where(
-        iota((crow, slot_l), 0) // picks == (iota((crow, slot_l), 1) % GRP) // CAP, mix, 0.0
-    )[:, :srow]
+        div(iota((crow, srow), 0), picks) == div(mod(iota((crow, srow), 1), GRP), CAP), mix, 0.0
+    )
     mix_hi = mix.astype(BF16)
     mix_lo = (mix - mix_hi.astype(F32)).astype(BF16)
+    home_r = iota((CUTS * own, rows), 0)
+    mine = iota((CUTS * own, rows), 1) == mod(home_r, own) + me_t * own
+    home = jnp.where(
+        div(iota((CUTS * own, crow), 0), own) == div(iota((CUTS * own, crow), 1), picks),
+        nt_dot(mine.astype(F32).astype(BF16), pick_b),
+        0.0,
+    ).astype(BF16)
     gain_copy.wait()
-    row_c = iota((GRP, chunk), 0) // CAP
+    row_c = div(iota((GRP, chunk), 0), CAP)
     spread_gain = jnp.broadcast_to(gain_v[:, :chunk], (GRP, chunk))
     for c in range(1, CUTS):
         spread_gain = jnp.where(
@@ -251,13 +265,13 @@
     square = jnp.sum(rows_x * rows_x, axis=1, keepdims=True)
     scaled = (rows_x.reshape(n_e, GRP, chunk) * gain_rows[...][None]).reshape(srow, chunk)
     up_all = nn_dot(scaled.astype(BF16), up_v[...])
-    own_c = (iota((srow, ff), 0) % GRP) // CAP
+    own_c = div(mod(iota((srow, ff), 0), GRP), CAP)
     up_own = up_all[:, :ff]
     for c in range(1, CUTS):
         up_own = jnp.where(own_c == c, up_all[:, c * ff : (c + 1) * ff], up_own)
     joined = jnp.concatenate([up_own, jnp.broadcast_to(square, (srow, ff))], axis=1)
     r_i, c_i = iota((srow, srow), 0), iota((srow, srow), 1)
-    same = ((r_i // GRP == c_i // GRP) & (r_i % CAP == c_i % CAP)).astype(F32)
+    same = ((div(r_i, GRP) == div(c_i, GRP)) & (mod(r_i, CAP) == mod(c_i, CAP))).astype(F32)
     summed = jnp.dot(same, joined, preferred_element_type=F32, precision=lax.Precision.HIGHEST)
     up_proj = summed[:, :ff] * lax.rsqrt(summed[:, ff:] * (1.0 / width) + 1e-06)
     hidden = up_proj / (1.0 + jnp.exp(-up_proj))
@@ -324,11 +338,6 @@
     for peer in t_peers:
         copy5(me_t, peer).start()
 
-    mine = spread[pl.ds(pl.multiple_of(me_t * own, own), own), :]
-    home = jnp.concatenate([mine] * CUTS, axis=0)
-    home = jnp.where(
-        iota((CUTS * own, pick_l), 0) // own == iota((CUTS * own, pick_l), 1) // picks, home, 0.0
-    )[:, :crow].astype(BF16)
     for peer in t_peers[::-1]:
         copy5(peer, me_t).wait_recv()
     for t in range(n_t):
@@ -369,12 +378,11 @@
         scratch_shapes=[
             pltpu.VMEM((CUTS * rows, chunk), BF16),
             pltpu.VMEM((1, width), F32),
-            pltpu.VMEM(expert_ids.shape, jnp.int32),
-            pltpu.VMEM(gate_values.shape, F32),
+            pltpu.VMEM(expert_ids.shape[::-1], jnp.int32),
+            pltpu.VMEM(gate_values.shape[::-1], F32),
             pltpu.VMEM((chunk, CUTS * ff), BF16),
             pltpu.VMEM((CUTS * ff, chunk), BF16),
             pltpu.VMEM((GRP, chunk), F32),
-            pltpu.VMEM((rows, max(128, crow)), F32),
             pltpu.VMEM((n_t, crow, lanes), BF16),
             pltpu.VMEM((n_t, crow, lanes), BF16),
             pltpu.VMEM((n_e, GRP, lanes), BF16),
@@ -399,9 +407,9 @@
             dma((n_t,)),
         ],
         compiler_params=pltpu.CompilerParams(
-            collective_id=0, has_side_effects=True, vmem_limit_bytes=48 * 1024 * 1024
+            collective_id=0, has_side_effects=True, vmem_limit_bytes=63 * 1024 * 1024
         ),
-    )(partials, norm_gain.reshape(1, width), expert_ids, gate_values, up_weight, down_weight)
+    )(partials, norm_gain.reshape(1, width), expert_ids.T, gate_values.T, up_weight, down_weight)
 
 
 def solution(mesh):

time: 36.2 us -> 31.2 us (0.86)
  local copies, waits for them, and re-layouts: 7.15 us -> 1.64 us
  Pallas kernels: 28.7 us -> 29.4 us
    unnamed x11 -> x1, local copies, waits for them, and re-layouts: 7.15 us -> 1.64 us
    pallas_call x1, Pallas kernels: 28.7 us -> 29.4 us  [on_device(): pl.pallas_call(functools.partial(kernel, (n_e, n_t, rows, width)), out_sh...]
where the time goes in v2:
time: 31.2 us; the launch traced here: 31 us
  Pallas kernels  29.4 us (94%)
  local copies, waits for them, and re-layouts  1.64 us (5%)
    pallas_call x1, Pallas kernels, on_device(): pl.pallas_call(functools.partial(kernel, (n_e, n_t, rows, width)), out_sh...  29.4 us
    unnamed x1, local copies, waits for them, and re-layouts  1.64 us

profile of v2, /device:TPU:0, one launch (start us, length us, event | category | flops | bytes accessed | tf_op | source)
XLA Modules:
  0.0 31.0 jit_solution(7345908317511582102)
XLA Ops:
  0.0 29.4 %shard_map.64 = bf16[16,7168]{1,0:T(8,128)(2,1)} custom-call(bf16[1,64,7168]{2,1,0:T(8,128)(2,1)} %part_hbm.1, f32[1,7168]{1,0:T(1,128)} %bitcast.3, s32[8,64]{1,0:T(8,128)} %bitcast.4, f32[8,64]{1,0:T(8,128)} %bitcast.5, bf16[1,7168,128]{2,1,0:T(8,128)(2,1)} %up_hbm.1, bf16[1,128,7168]{2,1,0:T(8,128)(2,1)} %down_hbm.1), custom_call_target="tpu_custom_call" | custom-call | tf_op jit(solution)/shard_map/pallas_call | solution.py:373
  29.4 1.6 %copy.8 = bf16[16,7168]{1,0:T(8,128)(2,1)} copy(bf16[16,7168]{1,0:T(8,128)(2,1)} %shard_map.64) | data formatting | bytes 458752

commit v3 on v2

--- a/solution.py
+++ b/solution.py
@@ -84,16 +84,27 @@
     srow = n_e * GRP
     me_e = lax.axis_index("expert")
     me_t = lax.axis_index("tensor")
+    n_x = n_t // 2
+    core, me_x = lax.rem(me_t, 2), lax.div(me_t, 2)
+    sibling = me_t + 1 - 2 * core
     t_order = sorted(range(1, n_t), key=lambda j: -min(j, n_t - j))
     e_order = sorted(range(1, n_e), key=lambda j: -min(j, n_e - j))
     t_peers = [lax.rem(me_t + j, n_t) for j in t_order]
     e_peers = [lax.rem(me_e + j, n_e) for j in e_order]
+    x_peers = [lax.rem(me_x + j, n_x) for j in range(1, n_x)]
+    far = [(e, x) for e in e_peers for x in x_peers + [me_x]] + [(me_e, x) for x in x_peers]
 
     barrier = pltpu.get_barrier_semaphore()
     for peer in t_peers:
         pl.semaphore_signal(barrier, inc=1, device_id={"tensor": peer}, device_id_type=MESH)
-    for peer in e_peers:
-        pl.semaphore_signal(barrier, inc=1, device_id={"expert": peer}, device_id_type=MESH)
+    for e in e_peers:
+        for x in x_peers + [me_x]:
+            pl.semaphore_signal(
+                barrier,
+                inc=1,
+                device_id={"expert": e, "tensor": 2 * x + core},
+                device_id_type=MESH,
+            )
 
     small = [
         pltpu.make_async_copy(ids_hbm, ids_v, load_sem.at[0]),
@@ -102,7 +113,7 @@
     parts = [
         pltpu.make_async_copy(
             part_hbm.at[0, :, pl.ds(c * chunk, chunk)],
-            part_v.at[pl.ds(c * rows, rows), :],
+            part_v.at[pl.ds(c * rows, rows), pl.ds(0, chunk)],
             load_sem.at[2 + c],
         )
         for c in range(CUTS)
@@ -119,13 +130,16 @@
     downs = [
         pltpu.make_async_copy(
             down_hbm.at[0, :, pl.ds(c * chunk, chunk)],
-            down_v.at[pl.ds(c * ff, ff), :],
+            down_v.at[pl.ds(c * ff, ff), pl.ds(0, chunk)],
             load_sem.at[3 + 2 * CUTS + c],
         )
         for c in range(CUTS)
     ]
-    for copy in small + parts + [gain_copy] + ups + downs:
+    for copy in small + parts:
         copy.start()
+    pad = n_t * lanes - chunk
+    part_v[:, chunk:] = jnp.zeros((CUTS * rows, pad), BF16)
+    down_v[:, chunk:] = jnp.zeros((CUTS * ff, pad), BF16)
     for copy in small:
         copy.wait()
 
@@ -154,14 +168,10 @@
 
     for copy in parts:
         copy.wait()
-    for t in range(n_t):
-        lo, hi = min(t * lanes, chunk), min((t + 1) * lanes, chunk)
-        if hi - lo < lanes:
-            send1[t] = jnp.zeros((crow, lanes), BF16)
-        if hi > lo:
-            send1[t, :, : hi - lo] = nn_dot(chooser, part_v[:, lo:hi]).astype(BF16)
-
-    pl.semaphore_wait(barrier, len(t_peers) + len(e_peers))
+    pl.semaphore_wait(barrier, len(t_peers) + len(e_peers) * n_x)
+
+    def cols(t):
+        return pl.ds(pl.multiple_of(t * lanes, 128), lanes)
 
     def copy1(src_t, dst_t):
         return pltpu.make_async_remote_copy(
@@ -174,7 +184,11 @@
         )
 
     for peer in t_peers:
+        send1[peer] = nn_dot(chooser, part_v[:, cols(peer)]).astype(BF16)
         copy1(me_t, peer).start()
+    for copy in [gain_copy] + ups + downs:
+        copy.start()
+    total = nn_dot(chooser, part_v[:, cols(me_t)])
 
     in_slot = jnp.where(rank == mod(slot_r, CAP).astype(F32), named, 0.0)
     to_slots = jnp.where(
@@ -212,7 +226,6 @@
         )
     gain_rows[...] = spread_gain
 
-    total = send1[me_t].astype(F32)
     for peer in t_peers:
         copy1(peer, me_t).wait_recv()
         total = total + recv1[peer].astype(F32)
@@ -222,44 +235,39 @@
         send2[e] = slots[e * GRP : (e + 1) * GRP]
 
     def xpart(b, t):
-        return xbuf.at[
-            pl.ds(pl.multiple_of(b * GRP, GRP), GRP), pl.ds(pl.multiple_of(t * lanes, 128), lanes)
-        ]
-
-    def copy2(src_e, dst_e):
+        return xbuf.at[pl.ds(pl.multiple_of(b * GRP, GRP), GRP), cols(t)]
+
+    def copy2(src_e, src_x, dst_e, dst_x):
         return pltpu.make_async_remote_copy(
             src_ref=send2.at[dst_e],
-            dst_ref=xpart(src_e, me_t),
-            send_sem=s2.at[dst_e],
-            recv_sem=r2.at[src_e],
-            device_id={"expert": dst_e},
-            device_id_type=MESH,
-        )
-
-    def copy2b(b, src_t, dst_t):
-        return pltpu.make_async_remote_copy(
-            src_ref=xpart(b, src_t),
-            dst_ref=xpart(b, src_t),
-            send_sem=s2b.at[b, dst_t],
-            recv_sem=r2b.at[b, src_t],
-            device_id={"tensor": dst_t},
-            device_id_type=MESH,
-        )
-
-    for peer in e_peers:
-        copy2(me_e, peer).start()
+            dst_ref=xpart(src_e, 2 * src_x + core),
+            send_sem=s2.at[dst_e, dst_x],
+            recv_sem=r2.at[src_e, src_x],
+            device_id={"expert": dst_e, "tensor": 2 * dst_x + core},
+            device_id_type=MESH,
+        )
+
+    def copy2b(b, x, src_core):
+        return pltpu.make_async_remote_copy(
+            src_ref=xpart(b, 2 * x + src_core),
+            dst_ref=xpart(b, 2 * x + src_core),
+            send_sem=s2b.at[b, x],
+            recv_sem=r2b.at[b, x],
+            device_id={"tensor": sibling},
+            device_id_type=MESH,
+        )
+
+    for e, x in far:
+        copy2(me_e, me_x, e, x).start()
     xpart(me_e, me_t)[...] = send2[me_e]
-    for peer in t_peers:
-        copy2b(me_e, me_t, peer).start()
-    for src in e_peers[::-1]:
-        copy2(src, me_e).wait_recv()
-        for peer in t_peers:
-            copy2b(src, me_t, peer).start()
+    copy2b(me_e, me_x, core).start()
+    for e, x in far[::-1]:
+        copy2(e, x, me_e, me_x).wait_recv()
+        copy2b(e, x, core).start()
     for copy in ups:
         copy.wait()
-    for src in t_peers[::-1]:
-        for b in [me_e] + e_peers[::-1]:
-            copy2b(b, src, me_t).wait_recv()
+    for e, x in [(me_e, me_x)] + far[::-1]:
+        copy2b(e, x, 1 - core).wait_recv()
 
     rows_x = xbuf[:, :chunk].astype(F32)
     square = jnp.sum(rows_x * rows_x, axis=1, keepdims=True)
@@ -281,47 +289,42 @@
     for copy in downs:
         copy.wait()
 
-    def copy3(src_t, dst_t):
-        return pltpu.make_async_remote_copy(
-            src_ref=send3.at[dst_t],
-            dst_ref=recv3.at[src_t],
-            send_sem=s3.at[dst_t],
-            recv_sem=r3.at[src_t],
-            device_id={"tensor": dst_t},
-            device_id_type=MESH,
-        )
-
-    for t in range(n_t):
-        lo, hi = min(t * lanes, chunk), min((t + 1) * lanes, chunk)
-        if hi - lo < lanes:
-            send3[t] = jnp.zeros((srow, lanes), BF16)
-        if hi > lo:
-            send3[t, :, : hi - lo] = nn_dot(spread_h, down_v[:, lo:hi]).astype(BF16)
-    for peer in t_peers:
-        copy3(me_t, peer).start()
-
-    total = send3[me_t].astype(F32)
-    for peer in t_peers[::-1]:
-        copy3(peer, me_t).wait_recv()
-        total = total + recv3[peer].astype(F32)
-    send4[...] = total.astype(BF16).reshape(n_e, GRP, lanes)
-
-    def copy4(src_e, dst_e):
-        return pltpu.make_async_remote_copy(
-            src_ref=send4.at[dst_e],
-            dst_ref=recv4.at[src_e],
-            send_sem=s4.at[dst_e],
-            recv_sem=r4.at[src_e],
-            device_id={"expert": dst_e},
-            device_id_type=MESH,
-        )
-
-    for peer in e_peers:
-        copy4(me_e, peer).start()
-    recv4[me_e] = send4[me_e]
-    for peer in e_peers[::-1]:
-        copy4(peer, me_e).wait_recv()
-    pairs = recv4[...].reshape(srow, lanes)
+    def copy3(x):
+        return pltpu.make_async_remote_copy(
+            src_ref=send3.at[x],
+            dst_ref=recv3.at[x],
+            send_sem=s3.at[x],
+            recv_sem=r3.at[x],
+            device_id={"tensor": sibling},
+            device_id_type=MESH,
+        )
+
+    def copy4(src_e, src_x, dst_e, dst_x):
+        return pltpu.make_async_remote_copy(
+            src_ref=send4.at[dst_x, dst_e],
+            dst_ref=recv4.at[src_x, src_e],
+            send_sem=s4.at[dst_e, dst_x],
+            recv_sem=r4.at[src_e, src_x],
+            device_id={"expert": dst_e, "tensor": 2 * dst_x + core},
+            device_id_type=MESH,
+        )
+
+    for x in x_peers + [me_x]:
+        send3[x] = nn_dot(spread_h, down_v[:, cols(2 * x + 1 - core)]).astype(BF16)
+        copy3(x).start()
+    kept = [nn_dot(spread_h, down_v[:, cols(2 * x + core)]) for x in x_peers + [me_x]]
+    for k, x in enumerate(x_peers + [me_x]):
+        copy3(x).wait_recv()
+        both = (kept[k] + recv3[x].astype(F32)).astype(BF16)
+        send4[x] = both.reshape(n_e, GRP, lanes)
+        for e in e_peers:
+            copy4(me_e, me_x, e, x).start()
+        if k < n_x - 1:
+            copy4(me_e, me_x, me_e, x).start()
+    recv4[me_x, me_e] = send4[me_x, me_e]
+    for e, x in far[::-1]:
+        copy4(e, x, me_e, me_x).wait_recv()
+    pairs = jnp.sum(recv4[...].astype(F32), axis=0).astype(BF16).reshape(srow, lanes)
     mixed = nn_dot(mix_hi, pairs) + nn_dot(mix_lo, pairs)
     recv5[me_t] = mixed.astype(BF16)
 
@@ -351,13 +354,14 @@
 
     for peer in t_peers:
         copy1(me_t, peer).wait_send()
-        copy3(me_t, peer).wait_send()
         copy5(me_t, peer).wait_send()
-        for b in [me_e] + e_peers:
-            copy2b(b, me_t, peer).wait_send()
-    for peer in e_peers:
-        copy2(me_e, peer).wait_send()
-        copy4(me_e, peer).wait_send()
+    for x in x_peers + [me_x]:
+        copy3(x).wait_send()
+    copy2b(me_e, me_x, core).wait_send()
+    for e, x in far:
+        copy2(me_e, me_x, e, x).wait_send()
+        copy2b(e, x, core).wait_send()
+        copy4(me_e, me_x, e, x).wait_send()
 
 
 def on_device(partials, norm_gain, expert_ids, gate_values, up_weight, down_weight):
@@ -369,6 +373,7 @@
     crow = CUTS * 2 * n_e
     srow = n_e * GRP
     own = rows // n_t
+    n_x = n_t // 2
     dma = pltpu.SemaphoreType.DMA
     return pl.pallas_call(
         functools.partial(kernel, (n_e, n_t, rows, width)),
@@ -376,33 +381,33 @@
         in_specs=[pl.BlockSpec(memory_space=pl.ANY)] * 6,
         out_specs=pl.BlockSpec(memory_space=pltpu.VMEM),
         scratch_shapes=[
-            pltpu.VMEM((CUTS * rows, chunk), BF16),
+            pltpu.VMEM((CUTS * rows, n_t * lanes), BF16),
             pltpu.VMEM((1, width), F32),
             pltpu.VMEM(expert_ids.shape[::-1], jnp.int32),
             pltpu.VMEM(gate_values.shape[::-1], F32),
             pltpu.VMEM((chunk, CUTS * ff), BF16),
-            pltpu.VMEM((CUTS * ff, chunk), BF16),
+            pltpu.VMEM((CUTS * ff, n_t * lanes), BF16),
             pltpu.VMEM((GRP, chunk), F32),
             pltpu.VMEM((n_t, crow, lanes), BF16),
             pltpu.VMEM((n_t, crow, lanes), BF16),
             pltpu.VMEM((n_e, GRP, lanes), BF16),
             pltpu.VMEM((srow, n_t * lanes), BF16),
-            pltpu.VMEM((n_t, srow, lanes), BF16),
-            pltpu.VMEM((n_t, srow, lanes), BF16),
-            pltpu.VMEM((n_e, GRP, lanes), BF16),
-            pltpu.VMEM((n_e, GRP, lanes), BF16),
+            pltpu.VMEM((n_x, srow, lanes), BF16),
+            pltpu.VMEM((n_x, srow, lanes), BF16),
+            pltpu.VMEM((n_x, n_e, GRP, lanes), BF16),
+            pltpu.VMEM((n_x, n_e, GRP, lanes), BF16),
             pltpu.VMEM((n_t, crow, lanes), BF16),
             dma((3 + 3 * CUTS,)),
             dma((n_t,)),
             dma((n_t,)),
-            dma((n_e,)),
-            dma((n_e,)),
-            dma((n_e, n_t)),
-            dma((n_e, n_t)),
-            dma((n_t,)),
-            dma((n_t,)),
-            dma((n_e,)),
-            dma((n_e,)),
+            dma((n_e, n_x)),
+            dma((n_e, n_x)),
+            dma((n_e, n_x)),
+            dma((n_e, n_x)),
+            dma((n_x,)),
+            dma((n_x,)),
+            dma((n_e, n_x)),
+            dma((n_e, n_x)),
             dma((n_t,)),
             dma((n_t,)),
         ],

time: 31.2 us -> 28.5 us (0.913)
  Pallas kernels: 29.4 us -> 26.6 us
    pallas_call x1, Pallas kernels: 29.4 us -> 26.6 us  [on_device(): pl.pallas_call(functools.partial(kernel, (n_e, n_t, rows, width)), out_sh...]
where the time goes in v3:
time: 28.5 us; the launch traced here: 28.3 us
  Pallas kernels  26.6 us (93%)
  local copies, waits for them, and re-layouts  1.64 us (6%)
    pallas_call x1, Pallas kernels, on_device(): pl.pallas_call(functools.partial(kernel, (n_e, n_t, rows, width)), out_sh...  26.6 us
    unnamed x1, local copies, waits for them, and re-layouts  1.64 us

profile of v3, /device:TPU:0, one launch (start us, length us, event | category | flops | bytes accessed | tf_op | source)
XLA Modules:
  0.0 28.3 jit_solution(8833098312140518272)
XLA Ops:
  0.0 26.6 %shard_map.64 = bf16[16,7168]{1,0:T(8,128)(2,1)} custom-call(bf16[1,64,7168]{2,1,0:T(8,128)(2,1)} %part_hbm.1, f32[1,7168]{1,0:T(1,128)} %bitcast.3, s32[8,64]{1,0:T(8,128)} %bitcast.4, f32[8,64]{1,0:T(8,128)} %bitcast.5, bf16[1,7168,128]{2,1,0:T(8,128)(2,1)} %up_hbm.1, bf16[1,128,7168]{2,1,0:T(8,128)(2,1)} %down_hbm.1), custom_call_target="tpu_custom_call" | custom-call | tf_op jit(solution)/shard_map/pallas_call | solution.py:378
  26.6 1.6 %copy.8 = bf16[16,7168]{1,0:T(8,128)(2,1)} copy(bf16[16,7168]{1,0:T(8,128)(2,1)} %shard_map.64) | data formatting | bytes 458752

commit v4 on v3

--- a/solution.py
+++ b/solution.py
@@ -25,6 +25,19 @@
 
 def mod(x, n):
     return x & (n - 1) if n & (n - 1) == 0 else x % n
+
+
+def partners(me, n):
+    if n & (n - 1):
+        return [lax.rem(me + j, n) for j in range(n - 1, 0, -1)]
+    flips = []
+    for j in range(n - 1, 0, -1):
+        other = me
+        for b in range(n.bit_length() - 1):
+            if j >> b & 1:
+                other = other + (1 << b) * (1 - 2 * lax.rem(lax.div(me, 1 << b), 2))
+        flips.append(other)
+    return flips
 
 
 def nt_dot(a, b):
@@ -87,11 +100,9 @@
     n_x = n_t // 2
     core, me_x = lax.rem(me_t, 2), lax.div(me_t, 2)
     sibling = me_t + 1 - 2 * core
-    t_order = sorted(range(1, n_t), key=lambda j: -min(j, n_t - j))
-    e_order = sorted(range(1, n_e), key=lambda j: -min(j, n_e - j))
-    t_peers = [lax.rem(me_t + j, n_t) for j in t_order]
-    e_peers = [lax.rem(me_e + j, n_e) for j in e_order]
-    x_peers = [lax.rem(me_x + j, n_x) for j in range(1, n_x)]
+    t_peers = partners(me_t, n_t)
+    e_peers = partners(me_e, n_e)
+    x_peers = partners(me_x, n_x)
     far = [(e, x) for e in e_peers for x in x_peers + [me_x]] + [(me_e, x) for x in x_peers]
 
     barrier = pltpu.get_barrier_semaphore()
@@ -171,7 +182,8 @@
     pl.semaphore_wait(barrier, len(t_peers) + len(e_peers) * n_x)
 
     def cols(t):
-        return pl.ds(pl.multiple_of(t * lanes, 128), lanes)
+        place = lax.rem(t, 2) * n_x + lax.div(t, 2)
+        return pl.ds(pl.multiple_of(place * lanes, 128), lanes)
 
     def copy1(src_t, dst_t):
         return pltpu.make_async_remote_copy(
@@ -247,12 +259,16 @@
             device_id_type=MESH,
         )
 
-    def copy2b(b, x, src_core):
-        return pltpu.make_async_remote_copy(
-            src_ref=xpart(b, 2 * x + src_core),
-            dst_ref=xpart(b, 2 * x + src_core),
-            send_sem=s2b.at[b, x],
-            recv_sem=r2b.at[b, x],
+    def copy2b(b, src_core):
+        part = xbuf.at[
+            pl.ds(pl.multiple_of(b * GRP, GRP), GRP),
+            pl.ds(pl.multiple_of(src_core * n_x * lanes, 128), n_x * lanes),
+        ]
+        return pltpu.make_async_remote_copy(
+            src_ref=part,
+            dst_ref=part,
+            send_sem=s2b.at[b],
+            recv_sem=r2b.at[b],
             device_id={"tensor": sibling},
             device_id_type=MESH,
         )
@@ -260,14 +276,15 @@
     for e, x in far:
         copy2(me_e, me_x, e, x).start()
     xpart(me_e, me_t)[...] = send2[me_e]
-    copy2b(me_e, me_x, core).start()
-    for e, x in far[::-1]:
-        copy2(e, x, me_e, me_x).wait_recv()
-        copy2b(e, x, core).start()
+    blocks = [me_e] + e_peers[::-1]
+    for b in blocks:
+        for x in x_peers[::-1] if b is me_e else [me_x] + x_peers[::-1]:
+            copy2(b, x, me_e, me_x).wait_recv()
+        copy2b(b, core).start()
     for copy in ups:
         copy.wait()
-    for e, x in [(me_e, me_x)] + far[::-1]:
-        copy2b(e, x, 1 - core).wait_recv()
+    for b in blocks:
+        copy2b(b, 1 - core).wait_recv()
 
     rows_x = xbuf[:, :chunk].astype(F32)
     square = jnp.sum(rows_x * rows_x, axis=1, keepdims=True)
@@ -344,7 +361,8 @@
     for peer in t_peers[::-1]:
         copy5(peer, me_t).wait_recv()
     for t in range(n_t):
-        lo, hi = min(t * lanes, chunk), min((t + 1) * lanes, chunk)
+        place = t % 2 * n_x + t // 2
+        lo, hi = min(place * lanes, chunk), min((place + 1) * lanes, chunk)
         if hi > lo:
             block = nn_dot(home, recv5[t]).astype(BF16)
             for c in range(CUTS):
@@ -357,10 +375,10 @@
         copy5(me_t, peer).wait_send()
     for x in x_peers + [me_x]:
         copy3(x).wait_send()
-    copy2b(me_e, me_x, core).wait_send()
+    for b in blocks:
+        copy2b(b, core).wait_send()
     for e, x in far:
         copy2(me_e, me_x, e, x).wait_send()
-        copy2b(e, x, core).wait_send()
         copy4(me_e, me_x, e, x).wait_send()
 
 
@@ -402,8 +420,8 @@
             dma((n_t,)),
             dma((n_e, n_x)),
             dma((n_e, n_x)),
-            dma((n_e, n_x)),
-            dma((n_e, n_x)),
+            dma((n_e,)),
+            dma((n_e,)),
             dma((n_x,)),
             dma((n_x,)),
             dma((n_e, n_x)),

time: 28.5 us -> 28.4 us (level)
  no operation moved by 1% of the time
where the time goes in v4:
time: 28.4 us; the launch traced here: 28.2 us
  Pallas kernels  26.6 us (94%)
  local copies, waits for them, and re-layouts  1.64 us (6%)
    pallas_call x1, Pallas kernels, on_device(): pl.pallas_call(functools.partial(kernel, (n_e, n_t, rows, width)), out_sh...  26.6 us
    unnamed x1, local copies, waits for them, and re-layouts  1.64 us

profile of v4, /device:TPU:0, one launch (start us, length us, event | category | flops | bytes accessed | tf_op | source)
XLA Modules:
  0.0 28.2 jit_solution(10279030500671919988)
XLA Ops:
  0.0 26.6 %shard_map.64 = bf16[16,7168]{1,0:T(8,128)(2,1)} custom-call(bf16[1,64,7168]{2,1,0:T(8,128)(2,1)} %part_hbm.1, f32[1,7168]{1,0:T(1,128)} %bitcast.3, s32[8,64]{1,0:T(8,128)} %bitcast.4, f32[8,64]{1,0:T(8,128)} %bitcast.5, bf16[1,7168,128]{2,1,0:T(8,128)(2,1)} %up_hbm.1, bf16[1,128,7168]{2,1,0:T(8,128)(2,1)} %down_hbm.1), custom_call_target="tpu_custom_call" | custom-call | tf_op jit(solution)/shard_map/pallas_call | solution.py:396
  26.6 1.6 %copy.8 = bf16[16,7168]{1,0:T(8,128)(2,1)} copy(bf16[16,7168]{1,0:T(8,128)(2,1)} %shard_map.64) | data formatting | bytes 458752

commit v5 on v4

--- a/solution.py
+++ b/solution.py
@@ -105,6 +105,38 @@
     x_peers = partners(me_x, n_x)
     far = [(e, x) for e in e_peers for x in x_peers + [me_x]] + [(me_e, x) for x in x_peers]
 
+    small = [
+        pltpu.make_async_copy(ids_hbm, ids_v, load_sem.at[0]),
+        pltpu.make_async_copy(gate_hbm, gate_v, load_sem.at[1]),
+    ]
+    parts = [
+        pltpu.make_async_copy(
+            part_hbm.at[0, :, pl.ds(c * chunk, chunk)],
+            part_v.at[pl.ds(c * rows, rows), pl.ds(0, chunk)],
+            load_sem.at[2 + c],
+        )
+        for c in range(CUTS)
+    ]
+    gain_copy = pltpu.make_async_copy(gain_hbm, gain_v, load_sem.at[2 + CUTS])
+    ups = [
+        pltpu.make_async_copy(
+            up_hbm.at[0, pl.ds(c * chunk, chunk), :],
+            up_v.at[:, pl.ds(c * ff, ff)],
+            load_sem.at[3 + CUTS + c],
+        )
+        for c in range(CUTS)
+    ]
+    downs = [
+        pltpu.make_async_copy(
+            down_hbm.at[0, :, pl.ds(c * chunk, chunk)],
+            down_v.at[pl.ds(c * ff, ff), pl.ds(0, chunk)],
+            load_sem.at[3 + 2 * CUTS + c],
+        )
+        for c in range(CUTS)
+    ]
+    for copy in small + parts:
+        copy.start()
+
     barrier = pltpu.get_barrier_semaphore()
     for peer in t_peers:
         pl.semaphore_signal(barrier, inc=1, device_id={"tensor": peer}, device_id_type=MESH)
@@ -117,37 +149,6 @@
                 device_id_type=MESH,
             )
 
-    small = [
-        pltpu.make_async_copy(ids_hbm, ids_v, load_sem.at[0]),
-        pltpu.make_async_copy(gate_hbm, gate_v, load_sem.at[1]),
-    ]
-    parts = [
-        pltpu.make_async_copy(
-            part_hbm.at[0, :, pl.ds(c * chunk, chunk)],
-            part_v.at[pl.ds(c * rows, rows), pl.ds(0, chunk)],
-            load_sem.at[2 + c],
-        )
-        for c in range(CUTS)
-    ]
-    gain_copy = pltpu.make_async_copy(gain_hbm, gain_v, load_sem.at[2 + CUTS])
-    ups = [
-        pltpu.make_async_copy(
-            up_hbm.at[0, pl.ds(c * chunk, chunk), :],
-            up_v.at[:, pl.ds(c * ff, ff)],
-            load_sem.at[3 + CUTS + c],
-        )
-        for c in range(CUTS)
-    ]
-    downs = [
-        pltpu.make_async_copy(
-            down_hbm.at[0, :, pl.ds(c * chunk, chunk)],
-            down_v.at[pl.ds(c * ff, ff), pl.ds(0, chunk)],
-            load_sem.at[3 + 2 * CUTS + c],
-        )
-        for c in range(CUTS)
-    ]
-    for copy in small + parts:
-        copy.start()
     pad = n_t * lanes - chunk
     part_v[:, chunk:] = jnp.zeros((CUTS * rows, pad), BF16)
     down_v[:, chunk:] = jnp.zeros((CUTS * ff, pad), BF16)
@@ -169,8 +170,7 @@
     picked = jnp.where(counts[:crow] == pick_r, any_hit, 0.0)
     pick_b = picked.astype(BF16)
     rank = counts[crow:]
-    repeat = iota((rows, CUTS * rows), 0) == mod(iota((rows, CUTS * rows), 1), rows)
-    wide = nn_dot(pick_b, repeat.astype(F32).astype(BF16))
+    wide = jnp.concatenate([picked] * CUTS, axis=1)
     chooser = jnp.where(
         div(iota((crow, CUTS * rows), 0), picks) == div(iota((crow, CUTS * rows), 1), rows),
         wide,
@@ -219,7 +219,8 @@
         div(iota((crow, srow), 0), picks) == div(mod(iota((crow, srow), 1), GRP), CAP), mix, 0.0
     )
     mix_hi = mix.astype(BF16)
-    mix_lo = (mix - mix_hi.astype(F32)).astype(BF16)
+    mix_lo = mix - mix_hi.astype(F32)
+    mix_two = jnp.concatenate([mix_hi.astype(F32), mix_lo], axis=1).astype(BF16)
     home_r = iota((CUTS * own, rows), 0)
     mine = iota((CUTS * own, rows), 1) == mod(home_r, own) + me_t * own
     home = jnp.where(
@@ -342,7 +343,7 @@
     for e, x in far[::-1]:
         copy4(e, x, me_e, me_x).wait_recv()
     pairs = jnp.sum(recv4[...].astype(F32), axis=0).astype(BF16).reshape(srow, lanes)
-    mixed = nn_dot(mix_hi, pairs) + nn_dot(mix_lo, pairs)
+    mixed = nn_dot(mix_two, jnp.concatenate([pairs, pairs], axis=0))
     recv5[me_t] = mixed.astype(BF16)
 
     def copy5(src_t, dst_t):

time: 28.4 us -> 28.4 us (level)
  no operation moved by 1% of the time
where the time goes in v5:
time: 28.4 us; the launch traced here: 28.2 us
  Pallas kernels  26.6 us (94%)
  local copies, waits for them, and re-layouts  1.64 us (6%)
    pallas_call x1, Pallas kernels, on_device(): pl.pallas_call(functools.partial(kernel, (n_e, n_t, rows, width)), out_sh...  26.6 us
    unnamed x1, local copies, waits for them, and re-layouts  1.64 us

profile of v5, /device:TPU:0, one launch (start us, length us, event | category | flops | bytes accessed | tf_op | source)
XLA Modules:
  0.0 28.2 jit_solution(12560649418874164281)
XLA Ops:
  0.0 26.6 %shard_map.64 = bf16[16,7168]{1,0:T(8,128)(2,1)} custom-call(bf16[1,64,7168]{2,1,0:T(8,128)(2,1)} %part_hbm.1, f32[1,7168]{1,0:T(1,128)} %bitcast.3, s32[8,64]{1,0:T(8,128)} %bitcast.4, f32[8,64]{1,0:T(8,128)} %bitcast.5, bf16[1,7168,128]{2,1,0:T(8,128)(2,1)} %up_hbm.1, bf16[1,128,7168]{2,1,0:T(8,128)(2,1)} %down_hbm.1), custom_call_target="tpu_custom_call" | custom-call | tf_op jit(solution)/shard_map/pallas_call | solution.py:397
  26.6 1.6 %copy.8 = bf16[16,7168]{1,0:T(8,128)(2,1)} copy(bf16[16,7168]{1,0:T(8,128)(2,1)} %shard_map.64) | data formatting | bytes 458752
